TPU v7x, 32 devices: a whole 2x2x4 slice. The times are simulated.
32 devices in a mesh: runner: 4 (over z), tile: 8 (over y, x, core).
Axes of the slice: x: 2, y: 2, z: 4, core: 2. Of those that a mesh axis runs over, the one named last changes fastest.
Arguments:
- prior_mean_fields: float32 [3, 64, 512], P(None, 'tile'), may hold values from -0.2 to 0.2
- ensemble_deviations: float32 [128, 3, 64, 512], P('runner', None, 'tile'), may hold values from -0.75 to 0.75
- obs_cell: int32 [8, 4, 256], P('tile', 'runner'), may hold values from 0 to 3071
- obs_value: float32 [8, 4, 256], P('tile', 'runner'), may hold values from -3 to 3
- obs_var: float32 [8, 4, 256], P('tile', 'runner'), may hold values from 0.02 to 0.2
Outputs:
- advanced: float32 [128, 3, 64, 512], P('runner', None, 'tile')
Inputs may be any that keep to these rules, and one draw needn't show every extreme that they name: obs_cell[t, s, o] numbers a value of slab (t, s) as field * 2 * 512 + row within the slab * 512 + column.
All inputs are finite; a program needn't handle non-finite values.
Results may differ from a plain program's by a relative error of at most 0.0001.
Values sent between devices are 32-bit elements; how exact they have to be, the bound alone decides.
A program may use at most 128 MiB of HBM per device.

v0:
```python
import jax
import jax.numpy as jnp
from jax import lax
from jax.sharding import PartitionSpec as P

DB_ITERS = 3


TIME_STEP = 0.25
CORIOLIS = 0.2


def padded_2(block, sides, width):
    for axis, dim in sides:
        count = lax.axis_size(axis)
        forward = [(i, i + 1) for i in range(count - 1)]
        forward.append((count - 1, 0))
        backward = [(target, source) for source, target in forward]
        low = lax.ppermute(
            lax.slice_in_dim(block, block.shape[dim] - width, None, axis=dim), axis, forward
        )
        high = lax.ppermute(lax.slice_in_dim(block, 0, width, axis=dim), axis, backward)
        block = jnp.concatenate([low, block, high], axis=dim)
    return block


def along_x(field):
    return (
        8.0 * (jnp.roll(field, -1, -1) - jnp.roll(field, 1, -1))
        - (jnp.roll(field, -2, -1) - jnp.roll(field, 2, -1))
    ) / 12.0


def along_y(padded):
    return (8.0 * (padded[:, 3:-1] - padded[:, 1:-3]) - (padded[:, 4:] - padded[:, :-4])) / 12.0


def tendency_padded(padded):
    height = padded[:, 0]
    east_speed = padded[:, 1]
    north_speed = padded[:, 2]
    column_depth = 1.0 + height
    flux_x = column_depth * east_speed
    flux_y = column_depth * north_speed
    east_mid = east_speed[:, 2:-2]
    north_mid = north_speed[:, 2:-2]
    height_rate = -(along_x(flux_x[:, 2:-2]) + along_y(flux_y))
    east_rate = (
        -(east_mid * along_x(east_mid) + north_mid * along_y(east_speed))
        + CORIOLIS * north_mid
        - along_x(height[:, 2:-2])
    )
    north_rate = (
        -(east_mid * along_x(north_mid) + north_mid * along_y(north_speed))
        - CORIOLIS * east_mid
        - along_y(height)
    )
    return jnp.stack([height_rate, east_rate, north_rate], axis=1)


def tendency_of(state_now):
    padded = padded_2(state_now, (("tile", 2),), 2)
    return tendency_padded(padded)


def runge_kutta_update(state_now):
    slope_one = tendency_of(state_now)
    slope_two = tendency_of(state_now + 0.5 * TIME_STEP * slope_one)
    slope_three = tendency_of(state_now + 0.5 * TIME_STEP * slope_two)
    slope_four = tendency_of(state_now + TIME_STEP * slope_three)
    return state_now + TIME_STEP / 6.0 * (
        slope_one + 2.0 * slope_two + 2.0 * slope_three + slope_four
    )


def symmetric_inverse(matrix, identity):
    sym = 0.5 * (matrix + matrix.T)
    return jax.scipy.linalg.cho_solve((jnp.linalg.cholesky(sym), True), identity)


def inverse_root(matrix, iterations):
    identity = jnp.eye(matrix.shape[0], dtype=matrix.dtype)
    square_root = matrix
    inverse_part = identity
    for _ in range(iterations):
        inv_square = symmetric_inverse(square_root, identity)
        inv_inverse = symmetric_inverse(inverse_part, identity)
        square_root, inverse_part = (
            0.5 * (square_root + inv_inverse),
            0.5 * (inverse_part + inv_square),
        )
    return inverse_part


def make_transform(gram_matrix, innovation, ensemble):
    identity = jnp.eye(ensemble, dtype=gram_matrix.dtype)
    matrix = identity + gram_matrix / (ensemble - 1.0)
    root = inverse_root(matrix, DB_ITERS)
    inner = jnp.dot(root, innovation, precision=lax.Precision.HIGHEST)
    weights = jnp.dot(root, inner, precision=lax.Precision.HIGHEST) / (ensemble - 1.0)
    return root + weights[:, None]


def correct_with_observations(flat_state, columns):
    member_mean = jnp.mean(flat_state, axis=0)
    return member_mean + jnp.einsum(
        "kc,km->mc", flat_state - member_mean, columns, precision=lax.Precision.HIGHEST
    )


def per_device(prior_mean_fields, ensemble_deviations, obs_cell, obs_value, obs_var):
    runner_count = lax.axis_size("runner")
    members_dev, field_count, tile_rows, columns = ensemble_deviations.shape
    ensemble = members_dev * runner_count
    slab_rows = tile_rows // runner_count
    integrate_ensemble_trajectory = runge_kutta_update(
        prior_mean_fields[None] + ensemble_deviations
    )
    cell_list = obs_cell[0, 0]
    obs_values = obs_value[0, 0]
    variance = obs_var[0, 0]
    slab_pieces = lax.all_to_all(
        integrate_ensemble_trajectory, "runner", split_axis=2, concat_axis=0, tiled=True
    )
    flat_state = slab_pieces.reshape(ensemble, -1)
    picked = jnp.take(flat_state, cell_list, axis=1)
    mean_obs = jnp.mean(picked, axis=0)
    anomaly = picked - mean_obs
    scaled = anomaly / variance
    gram_part = jnp.einsum("ko,lo->kl", scaled, anomaly, precision=lax.Precision.HIGHEST)
    innovation_part = jnp.einsum(
        "ko,o->k", scaled, obs_values - mean_obs, precision=lax.Precision.HIGHEST
    )
    gram_matrix, innovation = lax.psum((gram_part, innovation_part), ("runner", "tile"))
    ensemble_mixing_matrix = make_transform(gram_matrix, innovation, ensemble)
    updated_posterior_fields = correct_with_observations(
        flat_state, ensemble_mixing_matrix
    ).reshape(ensemble, field_count, slab_rows, columns)
    returned = lax.all_to_all(
        updated_posterior_fields, "runner", split_axis=0, concat_axis=2, tiled=True
    )
    return returned + TIME_STEP * tendency_of(returned)


def solution(mesh):
    placed = (
        P(None, "tile", None),
        P("runner", None, "tile", None),
        P("tile", "runner", None),
        P("tile", "runner", None),
        P("tile", "runner", None),
    )
    return jax.shard_map(
        per_device,
        mesh=mesh,
        in_specs=placed,
        out_specs=P("runner", None, "tile", None),
        check_vma=False,
    )
```

profile of v0, /device:TPU:29, one launch (start us, length us, event | category | flops | bytes accessed | tf_op | source)
XLA Modules:
  0.0 422.5 jit_solution(7954603476717491017)
XLA Ops:
  10.8 7.1 %collective-permute-done = f32[32,3,2,512]{3,0,2,1:T(8,128)S(1)} collective-permute-done((f32[32,3,2,512]{3,0,2,1:T(8,128)S(1)}, f32[32,3,2,512]{3,0,2,1:T(8,128)S(1)}, u32[]{:S(2)}, u32[]{:S(2)}) %collective-permute-start) | collective-permute-done | bytes 393248 | tf_op jit(solution)/shard_map/ppermute | solution.py:19
  17.9 2.7 collective-permute-done.1
  28.5 4.4 %collective-permute-done.2 = f32[32,3,2,512]{3,0,2,1:T(8,128)S(1)} collective-permute-done((f32[32,3,2,512]{3,0,2,1:T(8,128)S(1)}, f32[32,3,2,512]{3,0,2,1:T(8,128)S(1)}, u32[]{:S(2)}, u32[]{:S(2)}) %collective-permute-start.2) | collective-permute-done | bytes 393248 | tf_op jit(solution)/shard_map/ppermute | solution.py:19
  32.9 5.3 %collective-permute-done.3 = f32[32,3,2,512]{3,0,2,1:T(8,128)S(1)} collective-permute-done((f32[32,3,2,512]{3,0,2,1:T(8,128)S(1)}, f32[32,3,2,512]{3,0,2,1:T(8,128)S(1)}, u32[]{:S(2)}, u32[]{:S(2)}) %collective-permute-start.3) | collective-permute-done | bytes 393248 | tf_op jit(solution)/shard_map/ppermute | solution.py:22
  49.6 6.1 %collective-permute-done.5 = f32[32,3,2,512]{3,0,2,1:T(8,128)S(1)} collective-permute-done((f32[32,3,2,512]{3,0,2,1:T(8,128)S(1)}, f32[32,3,2,512]{3,0,2,1:T(8,128)S(1)}, u32[]{:S(2)}, u32[]{:S(2)}) %collective-permute-start.5) | collective-permute-done | bytes 393248 | tf_op jit(solution)/shard_map/ppermute | solution.py:22
  62.4 15.4 %collective-permute-start.7 = (f32[32,3,2,512]{3,0,2,1:T(8,128)S(1)}, f32[32,3,2,512]{3,0,2,1:T(8,128)S(1)}, u32[]{:S(2)}, u32[]{:S(2)}) collective-permute-start(f32[32,3,2,512]{3,0,2,1:T(8,128)S(1)} %get-tuple-element.35), channel_id=1, source_target_pairs={{1,0},{2,1},{3,2},{4,3},{5,4},{6,5},{7,6},{0,7},{9,8},{10,9},{11,1... | collective-permute-start | bytes 1179656 | tf_op jit(solution)/shard_map/ppermute | solution.py:22
  77.8 4.3 %collective-permute-done.7 = f32[32,3,2,512]{3,0,2,1:T(8,128)S(1)} collective-permute-done((f32[32,3,2,512]{3,0,2,1:T(8,128)S(1)}, f32[32,3,2,512]{3,0,2,1:T(8,128)S(1)}, u32[]{:S(2)}, u32[]{:S(2)}) %collective-permute-start.7) | collective-permute-done | bytes 393248 | tf_op jit(solution)/shard_map/ppermute | solution.py:22
  90.5 4.7 %all-to-all-start = ((f32[32,3,8,512]{3,0,1,2:T(8,128)}), f32[32,3,8,512]{3,0,1,2:T(8,128)S(1)}, u32[]{:S(2)}, u32[]{:S(2)}) async-start(f32[32,3,8,512]{3,0,1,2:T(8,128)} %copy.57), calls=%async_computation | async-start | bytes 3145728 | tf_op jit(solution)/shard_map/all_to_all | solution.py:122
  95.4 11.7 %cholesky.100 = f32[128,128]{1,0:T(8,128)S(1)} custom-call(f32[128,128]{1,0:T(8,128)S(1)} %fusion.245), custom_call_target="Cholesky" | custom-call | tf_op jit(solution)/shard_map/jit(cholesky)/cholesky | solution.py:78
  108.4 9.8 %custom-call.12 = f32[1,128,128]{1,2,0:T(8,128)S(1)} custom-call(f32[1,128,128]{2,1,0:T(8,128)S(1)} %fusion.226), custom_call_target="InvertDiagBlocksLowerTriangular" | custom-call | tf_op jit(solution)/shard_map/jit(_cho_solve)/triangular_solve | solution.py:78
  118.6 7.9 %all-to-all-done = f32[32,3,8,512]{3,0,1,2:T(8,128)S(1)} async-done(((f32[32,3,8,512]{3,0,1,2:T(8,128)}), f32[32,3,8,512]{3,0,1,2:T(8,128)S(1)}, u32[]{:S(2)}, u32[]{:S(2)}) %all-to-all-start) | async-done | bytes 1572896 | tf_op jit(solution)/shard_map/all_to_all | solution.py:122
  133.3 42.4 %psum.15 = f32[128]{0:T(128)S(1)} all-reduce(f32[128]{0:T(128)S(1)} %convolution_bitcast_fusion.2), channel_id=1, replica_groups=mesh['runner'=4,'tile'=8] {'runner','tile'}, use_global_device_ids=true, to_apply=%region_5.8 | all-reduce | flops 128 | bytes 1024 | tf_op jit(solution)/shard_map/psum | solution.py:134
  175.7 80.2 %all-reduce.2.cloned.1.call-done = f32[128,128]{0,1:T(8,128)} async-done(((f32[128,128]{0,1:T(8,128)}), f32[128,128]{0,1:T(8,128)}) %all-reduce.2.cloned.1.call-update) | async-done | bytes 65552 | tf_op jit(solution)/shard_map/psum | solution.py:134
  257.9 11.7 %cholesky.89 = f32[128,128]{1,0:T(8,128)S(1)} custom-call(f32[128,128]{1,0:T(8,128)S(1)} %fusion.248), custom_call_target="Cholesky" | custom-call | tf_op jit(solution)/shard_map/jit(cholesky)/cholesky | solution.py:78
  270.9 9.8 %custom-call.11 = f32[1,128,128]{1,2,0:T(8,128)S(1)} custom-call(f32[1,128,128]{2,1,0:T(8,128)S(1)} %fusion.225), custom_call_target="InvertDiagBlocksLowerTriangular" | custom-call | tf_op jit(solution)/shard_map/jit(_cho_solve)/triangular_solve | solution.py:78
  281.5 11.7 %cholesky.122 = f32[128,128]{1,0:T(8,128)S(1)} custom-call(f32[128,128]{1,0:T(8,128)S(1)} %fusion.237), custom_call_target="Cholesky" | custom-call | tf_op jit(solution)/shard_map/jit(cholesky)/cholesky | solution.py:78
  294.6 10.0 %custom-call.14 = f32[1,128,128]{1,2,0:T(8,128)S(1)} custom-call(f32[1,128,128]{2,1,0:T(8,128)S(1)} %fusion.228), custom_call_target="InvertDiagBlocksLowerTriangular" | custom-call | tf_op jit(solution)/shard_map/jit(_cho_solve)/triangular_solve | solution.py:78
  305.8 11.7 %cholesky.133 = f32[128,128]{1,0:T(8,128)S(1)} custom-call(f32[128,128]{1,0:T(8,128)S(1)} %fusion.233), custom_call_target="Cholesky" | custom-call | tf_op jit(solution)/shard_map/jit(cholesky)/cholesky | solution.py:78
  318.9 9.8 %custom-call.15 = f32[1,128,128]{1,2,0:T(8,128)S(1)} custom-call(f32[1,128,128]{2,1,0:T(8,128)S(1)} %fusion.229), custom_call_target="InvertDiagBlocksLowerTriangular" | custom-call | tf_op jit(solution)/shard_map/jit(_cho_solve)/triangular_solve | solution.py:78
  329.1 11.7 %cholesky.111 = f32[128,128]{1,0:T(8,128)S(1)} custom-call(f32[128,128]{1,0:T(8,128)S(1)} %fusion.241), custom_call_target="Cholesky" | custom-call | tf_op jit(solution)/shard_map/jit(cholesky)/cholesky | solution.py:78
  342.1 10.0 %custom-call.13 = f32[1,128,128]{1,2,0:T(8,128)S(1)} custom-call(f32[1,128,128]{2,1,0:T(8,128)S(1)} %fusion.227), custom_call_target="InvertDiagBlocksLowerTriangular" | custom-call | tf_op jit(solution)/shard_map/jit(_cho_solve)/triangular_solve | solution.py:78
  356.1 39.5 %all_to_all.33 = f32[128,3,2,512]{3,2,1,0:T(2,128)S(1)} all-to-all(f32[128,3,2,512]{3,2,1,0:T(2,128)S(1)} %reshape.67), channel_id=1, replica_groups=mesh['runner'=4,'tile'=8] {'runner'}, dimensions={0} | all-to-all | bytes 3145728 | tf_op jit(solution)/shard_map/all_to_all | solution.py:139
  397.6 6.9 %collective-permute-done.8 = f32[32,3,2,512]{3,0,2,1:T(8,128)S(1)} collective-permute-done((f32[32,3,2,512]{3,0,2,1:T(8,128)S(1)}, f32[32,3,2,512]{3,0,2,1:T(8,128)S(1)}, u32[]{:S(2)}, u32[]{:S(2)}) %collective-permute-start.8) | collective-permute-done | bytes 393248 | tf_op jit(solution)/shard_map/ppermute | solution.py:19
  404.5 3.3 collective-permute-done.9
  (208 shorter events, 69.8 us)
Async XLA Ops:
  8.9 9.0 %collective-permute-start = (f32[32,3,2,512]{3,0,2,1:T(8,128)S(1)}, f32[32,3,2,512]{3,0,2,1:T(8,128)S(1)}, u32[]{:S(2)}, u32[]{:S(2)}) collective-permute-start(f32[32,3,2,512]{3,0,2,1:T(8,128)S(1)} %get-tuple-element.40), channel_id=1, source_target_pairs={{0,1},{1,2},{2,3},{3,4},{4,5},{5,6},{6,7},{7,0},{8,9},{9,10},{10,1... | collective-permute-start | bytes 1179656 | tf_op jit(solution)/shard_map/ppermute | solution.py:19
  10.8 9.9 %collective-permute-start.1 = (f32[32,3,2,512]{3,0,2,1:T(8,128)S(1)}, f32[32,3,2,512]{3,0,2,1:T(8,128)S(1)}, u32[]{:S(2)}, u32[]{:S(2)}) collective-permute-start(f32[32,3,2,512]{3,0,2,1:T(8,128)S(1)} %get-tuple-element.41), channel_id=1, source_target_pairs={{1,0},{2,1},{3,2},{4,3},{5,4},{6,5},{7,6},{0,7},{9,8},{10,9},{11,1... | collective-permute-start | bytes 1179656 | tf_op jit(solution)/shard_map/ppermute | solution.py:22
  24.9 1.4 copy-start
  24.9 1.4 copy-start.1
  27.6 5.3 %collective-permute-start.2 = (f32[32,3,2,512]{3,0,2,1:T(8,128)S(1)}, f32[32,3,2,512]{3,0,2,1:T(8,128)S(1)}, u32[]{:S(2)}, u32[]{:S(2)}) collective-permute-start(f32[32,3,2,512]{3,0,2,1:T(8,128)S(1)} %get-tuple-element.38), channel_id=1, source_target_pairs={{0,1},{1,2},{2,3},{3,4},{4,5},{5,6},{6,7},{7,0},{8,9},{9,10},{10,1... | collective-permute-start | bytes 1179656 | tf_op jit(solution)/shard_map/ppermute | solution.py:19
  27.6 10.6 %collective-permute-start.3 = (f32[32,3,2,512]{3,0,2,1:T(8,128)S(1)}, f32[32,3,2,512]{3,0,2,1:T(8,128)S(1)}, u32[]{:S(2)}, u32[]{:S(2)}) collective-permute-start(f32[32,3,2,512]{3,0,2,1:T(8,128)S(1)} %get-tuple-element.39), channel_id=1, source_target_pairs={{1,0},{2,1},{3,2},{4,3},{5,4},{6,5},{7,6},{0,7},{9,8},{10,9},{11,1... | collective-permute-start | bytes 1179656 | tf_op jit(solution)/shard_map/ppermute | solution.py:22
  44.8 4.8 %collective-permute-start.4 = (f32[32,3,2,512]{3,0,2,1:T(8,128)S(1)}, f32[32,3,2,512]{3,0,2,1:T(8,128)S(1)}, u32[]{:S(2)}, u32[]{:S(2)}) collective-permute-start(f32[32,3,2,512]{3,0,2,1:T(8,128)S(1)} %get-tuple-element.36), channel_id=1, source_target_pairs={{0,1},{1,2},{2,3},{3,4},{4,5},{5,6},{6,7},{7,0},{8,9},{9,10},{10,1... | collective-permute-start | bytes 1179656 | tf_op jit(solution)/shard_map/ppermute | solution.py:19
  44.9 10.8 %collective-permute-start.5 = (f32[32,3,2,512]{3,0,2,1:T(8,128)S(1)}, f32[32,3,2,512]{3,0,2,1:T(8,128)S(1)}, u32[]{:S(2)}, u32[]{:S(2)}) collective-permute-start(f32[32,3,2,512]{3,0,2,1:T(8,128)S(1)} %get-tuple-element.37), channel_id=1, source_target_pairs={{1,0},{2,1},{3,2},{4,3},{5,4},{6,5},{7,6},{0,7},{9,8},{10,9},{11,1... | collective-permute-start | bytes 1179656 | tf_op jit(solution)/shard_map/ppermute | solution.py:22
  62.3 15.5 %collective-permute-start.6 = (f32[32,3,2,512]{3,0,2,1:T(8,128)S(1)}, f32[32,3,2,512]{3,0,2,1:T(8,128)S(1)}, u32[]{:S(2)}, u32[]{:S(2)}) collective-permute-start(f32[32,3,2,512]{3,0,2,1:T(8,128)S(1)} %get-tuple-element.34), channel_id=1, source_target_pairs={{0,1},{1,2},{2,3},{3,4},{4,5},{5,6},{6,7},{7,0},{8,9},{9,10},{10,1... | collective-permute-start | bytes 1179656 | tf_op jit(solution)/shard_map/ppermute | solution.py:19
  62.4 19.7 %collective-permute-start.7 = (f32[32,3,2,512]{3,0,2,1:T(8,128)S(1)}, f32[32,3,2,512]{3,0,2,1:T(8,128)S(1)}, u32[]{:S(2)}, u32[]{:S(2)}) collective-permute-start(f32[32,3,2,512]{3,0,2,1:T(8,128)S(1)} %get-tuple-element.35), channel_id=1, source_target_pairs={{1,0},{2,1},{3,2},{4,3},{5,4},{6,5},{7,6},{0,7},{9,8},{10,9},{11,1... | collective-permute-start | bytes 1179656 | tf_op jit(solution)/shard_map/ppermute | solution.py:22
  90.5 27.7 %copy-start.3 = (s32[1,1,256]{2,1,0:T(1,128)S(1)}, s32[1,1,256]{2,1,0:T(1,128)}, u32[]{:S(2)}) copy-start(s32[1,1,256]{2,1,0:T(1,128)} %param.10) | copy-start | bytes 3076
  90.5 35.9 %all-to-all-start = ((f32[32,3,8,512]{3,0,1,2:T(8,128)}), f32[32,3,8,512]{3,0,1,2:T(8,128)S(1)}, u32[]{:S(2)}, u32[]{:S(2)}) async-start(f32[32,3,8,512]{3,0,1,2:T(8,128)} %copy.57), calls=%async_computation | async-start | bytes 3145728 | tf_op jit(solution)/shard_map/all_to_all | solution.py:122
  95.2 160.6 %all-reduce.2.cloned.1.call-start = ((), (), s32[]{:S(2)}) async-start(), calls=%async_computation.2 | async-start | bytes 131072 | tf_op jit(solution)/shard_map/psum | solution.py:134
  130.2 1.4 copy-start.4
  130.2 1.4 copy-start.5
  255.8 49.0 %copy-start.2 = (f32[128,128]{0,1:T(8,128)S(1)}, f32[128,128]{0,1:T(8,128)}, u32[]{:S(2)}) copy-start(f32[128,128]{0,1:T(8,128)} %all-reduce.2.cloned.1.call-done) | copy-start | bytes 196612
  396.0 8.5 %collective-permute-start.8 = (f32[32,3,2,512]{3,0,2,1:T(8,128)S(1)}, f32[32,3,2,512]{3,0,2,1:T(8,128)S(1)}, u32[]{:S(2)}, u32[]{:S(2)}) collective-permute-start(f32[32,3,2,512]{3,0,2,1:T(8,128)S(1)} %get-tuple-element.32), channel_id=1, source_target_pairs={{0,1},{1,2},{2,3},{3,4},{4,5},{5,6},{6,7},{7,0},{8,9},{9,10},{10,1... | collective-permute-start | bytes 1179656 | tf_op jit(solution)/shard_map/ppermute | solution.py:19
  397.6 10.2 %collective-permute-start.9 = (f32[32,3,2,512]{3,0,2,1:T(8,128)S(1)}, f32[32,3,2,512]{3,0,2,1:T(8,128)S(1)}, u32[]{:S(2)}, u32[]{:S(2)}) collective-permute-start(f32[32,3,2,512]{3,0,2,1:T(8,128)S(1)} %get-tuple-element.33), channel_id=1, source_target_pairs={{1,0},{2,1},{3,2},{4,3},{5,4},{6,5},{7,6},{0,7},{9,8},{10,9},{11,1... | collective-permute-start | bytes 1179656 | tf_op jit(solution)/shard_map/ppermute | solution.py:22
Sparse Core Ops, SparseCore 0:
  133.0 122.7 all-reduce.1
where the time goes:
time: 428 us; the launch traced here: 423 us
  other arithmetic  139 us (32%)
  waiting for transfers between devices  131 us (31%)
  blocking collectives  81.9 us (19%)
  starting transfers between devices  26.6 us (6%)
  local copies, waits for them, and re-layouts  23.7 us (6%)
  between operations  14.7 us (3%)
  matrix products  6.17 us (1%)
    psum x1, waiting for transfers between devices, per_device(): lax.psum((gram_part, innovation_part), ('runner', 'tile'))  80.2 us
    another operation x15, other arithmetic, symmetric_inverse(): jnp.linalg.cholesky(sym)  62 us
    another operation x10, other arithmetic, symmetric_inverse(): jax.scipy.linalg.cho_solve((jnp.linalg.cholesky(sym), True), identity)  52.6 us
    psum x1, blocking collectives, per_device(): lax.psum((gram_part, innovation_part), ('runner', 'tile'))  42.4 us
    all_to_all x1, blocking collectives, per_device(): lax.all_to_all(updated_posterior_fields, 'runner', split_axis=0, concat_a...  39.5 us
    ppermute x5, waiting for transfers between devices, padded_2(): lax.ppermute(lax.slice_in_dim(block, 0, width, axis=dim), axis, backward)  21.7 us
    ppermute x5, waiting for transfers between devices, padded_2(): lax.ppermute(lax.slice_in_dim(block, block.shape[dim] - width, None, axis...  21 us
    ppermute x5, starting transfers between devices, padded_2(): lax.ppermute(lax.slice_in_dim(block, 0, width, axis=dim), axis, backward)  18.4 us
  transfers between devices with their start and end apart: 12, of which 11 were waited for; matrix products, arithmetic and copies ran while one was open for 6% of the time, Pallas kernels for 0%

commit v1 on v0

v1 whole, which is shorter than its diff:
```python
import functools

import jax
import jax.numpy as jnp
import numpy as np
from jax import lax
from jax.experimental import pallas as pl
from jax.experimental.pallas import tpu as pltpu
from jax.sharding import PartitionSpec as P

TIME_STEP = 0.25
CORIOLIS = 0.2
MESH_ID = pl.DeviceIdType.MESH
HIGH = lax.Precision.HIGHEST


def root_terms():
    shifts = [0.0, 1.0, 3.0 - 2.0 * np.sqrt(2.0), 3.0 + 2.0 * np.sqrt(2.0)]
    weights = []
    for shift in shifts:
        at = -shift
        top = at**4 + 28 * at**3 + 70 * at**2 + 28 * at + 1
        bottom = 8.0
        for other in shifts:
            if other != shift:
                bottom *= at + other
        weights.append(top / bottom)
    return [float(s) for s in shifts], [float(w) for w in weights]


def along_x(field):
    width = field.shape[-1]
    axis = field.ndim - 1
    near = pltpu.roll(field, width - 1, axis) - pltpu.roll(field, 1, axis)
    far = pltpu.roll(field, width - 2, axis) - pltpu.roll(field, 2, axis)
    return near * (8.0 / 12.0) - far * (1.0 / 12.0)


def along_y(rows):
    return (rows[3] - rows[1]) * (8.0 / 12.0) - (rows[4] - rows[0]) * (1.0 / 12.0)


def tendency_row(load):
    e = [load(d, 0) for d in range(-2, 3)]
    u = [load(d, 1) for d in range(-2, 3)]
    v = [load(d, 2) for d in range(-2, 3)]
    flux_y = [(1.0 + e[d]) * v[d] if d != 2 else None for d in range(5)]
    flux_x = (1.0 + e[2]) * u[2]
    rate_e = -(along_x(flux_x) + along_y(flux_y))
    rate_u = -(u[2] * along_x(u[2]) + v[2] * along_y(u)) + CORIOLIS * v[2] - along_x(e[2])
    rate_v = -(u[2] * along_x(v[2]) + v[2] * along_y(v)) - CORIOLIS * u[2] - along_y(e)
    return rate_e, rate_u, rate_v


def kernel(
    R, T,
    x0, cell, val, var, out,
    pad, own, slab, cells, picks, picked, parts, part_in, run_in, gram_all, inv, mixed, back,
    halo_s, halo_r, cell_s, cell_r, pick_s, pick_r, g1_s, g1_r, g2_s, g2_r, g3_s, g3_r,
    slab_s, slab_r, back_s, back_r, last_s, last_r,
):
    r = lax.axis_index("runner")
    t = lax.axis_index("tile")
    chunks, rows, fields, mch, C = x0.shape
    M = chunks * mch
    E = M * R
    S = rows // R
    obs = cell.shape[-1]
    h = E // T
    up = lax.rem(t + 1, T)
    down = lax.rem(t + T - 1, T)

    def peer(axis, k):
        return lax.rem((r if axis == "runner" else t) + k, R if axis == "runner" else T)

    def copy(src, dst, send, recv, axis, to):
        return pltpu.make_async_remote_copy(
            src_ref=src, dst_ref=dst, send_sem=send, recv_sem=recv,
            device_id={axis: to}, device_id_type=MESH_ID,
        )

    barrier = pltpu.get_barrier_semaphore()
    for k in range(1, R):
        pl.semaphore_signal(barrier, inc=1, device_id={"runner": peer("runner", k)}, device_id_type=MESH_ID)
    for k in range(1, T):
        pl.semaphore_signal(barrier, inc=1, device_id={"tile": peer("tile", k)}, device_id_type=MESH_ID)
    pl.semaphore_wait(barrier, R - 1 + T - 1)

    cell_copies = [
        copy(cell, cells.at[r], cell_s.at[k - 1], cell_r.at[k - 1], "runner", peer("runner", k))
        for k in range(1, R)
    ]

    def halos(s, c):
        return (
            copy(pad.at[s, c, pl.ds(2, 2)], pad.at[s, c, pl.ds(rows + 2, 2)],
                 halo_s.at[s, 0, c], halo_r.at[s, 0, c], "tile", down),
            copy(pad.at[s, c, pl.ds(rows, 2)], pad.at[s, c, pl.ds(0, 2)],
                 halo_s.at[s, 1, c], halo_r.at[s, 1, c], "tile", up),
        )

    def begin(c, _):
        pad[0, c, pl.ds(2, rows)] = x0[c]
        for one in halos(0, c):
            one.start()
        return 0

    lax.fori_loop(0, chunks, begin, 0)
    for one in cell_copies:
        one.start()
    cells[r] = cell[...]

    for s in range(4):
        weight = TIME_STEP / 6.0 * (1.0 if s in (0, 3) else 2.0)
        ahead = TIME_STEP * (1.0 if s == 2 else 0.5)

        def stage(c, _, s=s, weight=weight, ahead=ahead):
            for one in halos(s, c):
                one.wait_recv()

            def one_row(j, _):
                rates = tendency_row(lambda d, f: pad[s, c, j + 2 + d, f])
                for f, rate in enumerate(rates):
                    if s == 0:
                        own[c, j, f] = x0[c, j, f] + weight * rate
                    else:
                        own[c, j, f] = own[c, j, f] + weight * rate
                    if s < 3:
                        pad[s + 1, c, j + 2, f] = x0[c, j, f] + ahead * rate
                return 0

            lax.fori_loop(0, rows, one_row, 0)
            if s < 3:
                for one in halos(s + 1, c):
                    one.start()
            return 0

        lax.fori_loop(0, chunks, stage, 0)

    for one in cell_copies:
        one.wait_recv()
    column = lax.broadcasted_iota(jnp.int32, (C, obs), 0)

    def pick(q, _):
        numbers = cells[q]
        total = jnp.zeros((3 * M, obs), jnp.float32)
        for j in range(S):
            for f in range(fields):
                value = own[:, q * S + j, f].reshape(M, C)
                first = value.astype(jnp.bfloat16)
                rest = value - first.astype(jnp.float32)
                second = rest.astype(jnp.bfloat16)
                third = (rest - second.astype(jnp.float32)).astype(jnp.bfloat16)
                hot = jnp.where(column == numbers - (f * S + j) * C, 1.0, 0.0).astype(jnp.bfloat16)
                total = total + jnp.dot(
                    jnp.concatenate([first, second, third], axis=0), hot,
                    preferred_element_type=jnp.float32,
                )
        picks[q] = total[:M] + total[M : 2 * M] + total[2 * M :]
        return 0

    lax.fori_loop(0, R, pick, 0)
    pick_copies = [
        copy(picks.at[peer("runner", k)], picked.at[r], pick_s.at[k - 1], pick_r.at[k - 1],
             "runner", peer("runner", k))
        for k in range(1, R)
    ]
    for one in pick_copies:
        one.start()
    picked[r] = picks[r]
    for one in pick_copies:
        one.wait_recv()

    seen = picked[...].reshape(E, obs)
    mean = jnp.sum(seen, axis=0, keepdims=True) * (1.0 / E)
    anomaly = seen - mean
    scaled = anomaly / var[...]
    gram = lax.dot_general(
        scaled, anomaly, (((1,), (1,)), ((), ())), precision=HIGH, preferred_element_type=jnp.float32
    )
    innovation = jnp.sum(scaled * (val[...] - mean), axis=1, keepdims=True)
    parts[:, :, :E] = gram.reshape(T, h, E)
    parts[:, :, E:] = jnp.broadcast_to(innovation, (E, 128)).reshape(T, h, 128)

    first_copies = [
        copy(parts.at[peer("tile", k)], part_in.at[t], g1_s.at[k - 1], g1_r.at[k - 1], "tile", peer("tile", k))
        for k in range(1, T)
    ]
    for one in first_copies:
        one.start()
    part_in[t] = parts[t]
    for one in first_copies:
        one.wait_recv()
    run_in[r] = jnp.sum(part_in[...], axis=0)
    second_copies = [
        copy(run_in.at[r], run_in.at[r], g2_s.at[k - 1], g2_r.at[k - 1], "runner", peer("runner", k))
        for k in range(1, R)
    ]
    for one in second_copies:
        one.start()
    for one in second_copies:
        one.wait_recv()
    gram_all[t] = jnp.sum(run_in[...], axis=0)
    third_copies = [
        copy(gram_all.at[t], gram_all.at[t], g3_s.at[k - 1], g3_r.at[k - 1], "tile", peer("tile", k))
        for k in range(1, T)
    ]
    for one in third_copies:
        one.start()

    slab_copies = [
        copy(own.at[:, pl.ds(peer("runner", k) * S, S)], slab.at[r], slab_s.at[k - 1], slab_r.at[k - 1],
             "runner", peer("runner", k))
        for k in range(1, R)
    ]
    for one in slab_copies:
        one.start()
    slab[r] = own[:, pl.ds(r * S, S)]
    for one in third_copies:
        one.wait_recv()

    total = gram_all[...].reshape(E, E + 128)
    eye = jnp.where(
        lax.broadcasted_iota(jnp.int32, (E, E), 0) == lax.broadcasted_iota(jnp.int32, (E, E), 1), 1.0, 0.0
    )
    shifts, weights = root_terms()
    for i, shift in enumerate(shifts):
        inv[i] = total[:, :E] * (1.0 / (E - 1.0)) + (1.0 + shift) * eye
    lane = lax.broadcasted_iota(jnp.int32, (1, E), 1)

    def sweep(k, _):
        here = lane == k
        for i in range(len(shifts)):
            now = inv[i]
            row = inv[i, pl.ds(k, 1), :]
            col = jnp.sum(jnp.where(here, now, 0.0), axis=1, keepdims=True)
            pivot = 1.0 / jnp.sum(jnp.where(here, row, 0.0), axis=1, keepdims=True)
            row = jnp.where(here, -pivot, row * pivot)
            inv[i] = jnp.where(here, 0.0, now) - col * row
            inv[i, pl.ds(k, 1), :] = row
        return 0

    lax.fori_loop(0, E, sweep, 0)
    root = 0.125 * eye
    for i, weight in enumerate(weights):
        root = root - weight * inv[i]
    inner = jnp.dot(root, total[:, E:], precision=HIGH, preferred_element_type=jnp.float32)
    extra = jnp.dot(root, inner, precision=HIGH, preferred_element_type=jnp.float32) * (1.0 / (E - 1.0))
    transform = root + extra[:, :1]
    transform = transform - jnp.sum(transform, axis=0, keepdims=True) * (1.0 / E) + 1.0 / E
    turned = transform.T

    for one in slab_copies:
        one.wait_recv()
    back_copies = [
        copy(mixed.at[peer("runner", k)], back.at[pl.ds(2 + r * S, S)], back_s.at[k - 1], back_r.at[k - 1],
             "runner", peer("runner", k))
        for k in range(1, R)
    ]
    for j in range(S):
        for f in range(fields):
            value = slab[:, :, j, f].reshape(E, C)
            result = jnp.dot(turned, value, precision=HIGH, preferred_element_type=jnp.float32)
            mixed[:, j, f] = result.reshape(R, M, C)
    for one in back_copies:
        one.start()
    back[pl.ds(2 + r * S, S)] = mixed[r]
    for one in back_copies:
        one.wait_recv()

    last_copies = [
        copy(back.at[pl.ds(2, 2)], back.at[pl.ds(rows + 2, 2)], last_s.at[0], last_r.at[0], "tile", down),
        copy(back.at[pl.ds(rows, 2)], back.at[pl.ds(0, 2)], last_s.at[1], last_r.at[1], "tile", up),
    ]
    for one in last_copies:
        one.start()
    for one in last_copies:
        one.wait_recv()

    def last_row(n, _):
        j = n // chunks
        members = pl.ds(pl.multiple_of((n % chunks) * mch, mch), mch)
        rates = tendency_row(lambda d, f: back[j + 2 + d, f, members, :])
        for f, rate in enumerate(rates):
            out[j, f, members, :] = back[j + 2, f, members, :] + TIME_STEP * rate
        return 0

    lax.fori_loop(0, rows * chunks, last_row, 0)

    def drain(c, _):
        for s in range(4):
            for one in halos(s, c):
                one.wait_send()
        return 0

    lax.fori_loop(0, chunks, drain, 0)
    for group in (cell_copies, pick_copies, first_copies, second_copies, third_copies,
                  slab_copies, back_copies, last_copies):
        for one in group:
            one.wait_send()


def per_device(R, T, prior_mean_fields, ensemble_deviations, obs_cell, obs_value, obs_var):
    M, fields, rows, C = ensemble_deviations.shape
    E = M * R
    S = rows // R
    mch = 8
    chunks = M // mch
    obs = obs_cell.shape[-1]
    h = E // T
    start = prior_mean_fields[None] + ensemble_deviations
    start = start.reshape(chunks, mch, fields, rows, C).transpose(0, 3, 2, 1, 4)
    f32 = jnp.float32
    dma = pltpu.SemaphoreType.DMA
    vmem = pl.BlockSpec(memory_space=pltpu.VMEM)
    pairs = lambda n: [dma((n,)), dma((n,))]
    result = pl.pallas_call(
        functools.partial(kernel, R, T),
        out_shape=jax.ShapeDtypeStruct((rows, fields, M, C), f32),
        in_specs=[vmem] * 4,
        out_specs=vmem,
        scratch_shapes=[
            pltpu.VMEM((4, chunks, rows + 4, fields, mch, C), f32),
            pltpu.VMEM((chunks, rows, fields, mch, C), f32),
            pltpu.VMEM((R, chunks, S, fields, mch, C), f32),
            pltpu.VMEM((R, 1, obs), jnp.int32),
            pltpu.VMEM((R, M, obs), f32),
            pltpu.VMEM((R, M, obs), f32),
            pltpu.VMEM((T, h, E + 128), f32),
            pltpu.VMEM((T, h, E + 128), f32),
            pltpu.VMEM((R, h, E + 128), f32),
            pltpu.VMEM((T, h, E + 128), f32),
            pltpu.VMEM((4, E, E), f32),
            pltpu.VMEM((R, S, fields, M, C), f32),
            pltpu.VMEM((rows + 4, fields, M, C), f32),
            dma((4, 2, chunks)), dma((4, 2, chunks)),
            *pairs(R - 1), *pairs(R - 1), *pairs(T - 1), *pairs(R - 1), *pairs(T - 1),
            *pairs(R - 1), *pairs(R - 1), *pairs(2),
        ],
        compiler_params=pltpu.CompilerParams(
            collective_id=0, has_side_effects=True, vmem_limit_bytes=48 * 1024 * 1024
        ),
        name="forecast",
    )(start, obs_cell[0], obs_value[0], obs_var[0])
    return result.transpose(2, 1, 0, 3)


def solution(mesh):
    placed = (
        P(None, "tile", None),
        P("runner", None, "tile", None),
        P("tile", "runner", None),
        P("tile", "runner", None),
        P("tile", "runner", None),
    )
    return jax.shard_map(
        functools.partial(per_device, mesh.shape["runner"], mesh.shape["tile"]),
        mesh=mesh,
        in_specs=placed,
        out_specs=P("runner", None, "tile", None),
        check_vma=False,
    )
```

time: 428 us -> 165 us (0.39)
  Pallas kernels: 0 us -> 159 us
  other arithmetic: 139 us -> 1.57 us
  waiting for transfers between devices: 131 us -> 0 us
  blocking collectives: 81.9 us -> 0 us
  starting transfers between devices: 26.6 us -> 0 us
  local copies, waits for them, and re-layouts: 23.7 us -> 2.99 us
  between operations: 14.7 us -> 0.07 us
  matrix products: 6.17 us -> 0 us
    pallas_call x0 -> x1, Pallas kernels: none -> 159 us  [per_device(): pl.pallas_call(functools.partial(kernel, R, T), out_shape=jax.ShapeDtypeS...]
    another operation x40 -> x0, other arithmetic: 124 us -> none  [the longest x15 62 us: symmetric_inverse(): jnp.linalg.cholesky(sym)]
    psum x1 -> x0, waiting for transfers between devices: 80.2 us -> none  [per_device(): lax.psum((gram_part, innovation_part), ('runner', 'tile'))]
    ppermute x10 -> x0, waiting for transfers between devices: 42.7 us -> none  [the longest x5 21.7 us: padded_2(): lax.ppermute(lax.slice_in_dim(block, 0, width, axis=dim), axis, backward)]
    psum x1 -> x0, blocking collectives: 42.4 us -> none  [per_device(): lax.psum((gram_part, innovation_part), ('runner', 'tile'))]
    all_to_all x1 -> x0, blocking collectives: 39.5 us -> none  [per_device(): lax.all_to_all(updated_posterior_fields, 'runner', split_axis=0, concat_a...]
    ppermute x10 -> x0, starting transfers between devices: 22 us -> none  [the longest x5 18.4 us: padded_2(): lax.ppermute(lax.slice_in_dim(block, 0, width, axis=dim), axis, backward)]
    slice x81 -> x0, local copies, waits for them, and re-layouts: 12.5 us -> none  [the longest x38 6.11 us: along_x(): jnp.roll(field, 1, -1)]
  transfers between devices with their start and end apart: 12 -> 0, of which waited for: 11 -> 0; matrix products, arithmetic and copies ran while one was open for 6% -> 0% of each run, Pallas kernels for 0% -> 0%
where the time goes in v1:
time: 165 us; the launch traced here: 164 us
  Pallas kernels  159 us (96%)
  local copies, waits for them, and re-layouts  2.99 us (2%)
    pallas_call x1, Pallas kernels, per_device(): pl.pallas_call(functools.partial(kernel, R, T), out_shape=jax.ShapeDtypeS...  159 us

profile of v1, /device:TPU:29, one launch (start us, length us, event | category | flops | bytes accessed | tf_op | source)
XLA Modules:
  0.0 163.7 jit_solution(14296504432463753625)
XLA Ops:
  0.0 1.6 broadcast_add_fusion
  1.6 0.0 copy-start
  1.6 0.0 copy-start.1
  1.6 0.0 copy-start.2
  1.6 0.9 copy.10
  2.5 0.0 copy-done
  2.5 0.0 copy-done.1
  2.6 0.0 copy-done.2
  2.6 159.1 %forecast.1 = f32[8,3,32,512]{3,2,1,0:T(8,128)S(1)} custom-call(f32[4,8,3,8,512]{4,3,2,1,0:T(8,128)S(1)} %bitcast.8, s32[1,256]{1,0:T(1,128)S(1)} %bitcast.10, f32[1,256]{1,0:T(1,128)S(1)} %bitcast.11, f32[1,256]{1,0:T(1,128)S(1)} %bitcast.12), custom_call_target="tpu_custom_call" | custom-call | tf_op jit(solution)/shard_map/forecast/pallas_call | solution.py:317
  161.6 2.1 %copy.8 = f32[32,3,8,512]{3,2,1,0:T(8,128)} copy(f32[32,3,8,512]{3,0,1,2:T(8,128)S(1)} %bitcast.9) | data formatting | bytes 3145728 | tf_op jit(solution)/shard_map/transpose | solution.py:345
Async XLA Ops:
  1.6 1.0 copy-start
  1.6 1.0 copy-start.1
  1.6 1.0 copy-start.2

commit v2 on v1

--- a/solution.py
+++ b/solution.py
@@ -99,6 +99,23 @@
                  halo_s.at[s, 1, c], halo_r.at[s, 1, c], "tile", up),
         )
 
+    def slab_copies(c):
+        return [
+            copy(own.at[c, pl.ds(peer("runner", k) * S, S)], slab.at[r, c], slab_s.at[k - 1, c],
+                 slab_r.at[k - 1, c], "runner", peer("runner", k))
+            for k in range(1, R)
+        ]
+
+    def start_slabs(c, _):
+        for one in slab_copies(c):
+            one.start()
+        return 0
+
+    def wait_slabs(c, _):
+        for one in slab_copies(c):
+            one.wait_recv()
+        return 0
+
     def begin(c, _):
         pad[0, c, pl.ds(2, rows)] = x0[c]
         for one in halos(0, c):
@@ -133,6 +150,8 @@
             if s < 3:
                 for one in halos(s + 1, c):
                     one.start()
+            else:
+                slab[r, c] = own[c, pl.ds(r * S, S)]
             return 0
 
         lax.fori_loop(0, chunks, stage, 0)
@@ -208,14 +227,7 @@
     for one in third_copies:
         one.start()
 
-    slab_copies = [
-        copy(own.at[:, pl.ds(peer("runner", k) * S, S)], slab.at[r], slab_s.at[k - 1], slab_r.at[k - 1],
-             "runner", peer("runner", k))
-        for k in range(1, R)
-    ]
-    for one in slab_copies:
-        one.start()
-    slab[r] = own[:, pl.ds(r * S, S)]
+    lax.fori_loop(0, chunks, start_slabs, 0)
     for one in third_copies:
         one.wait_recv()
 
@@ -227,20 +239,32 @@
     for i, shift in enumerate(shifts):
         inv[i] = total[:, :E] * (1.0 / (E - 1.0)) + (1.0 + shift) * eye
     lane = lax.broadcasted_iota(jnp.int32, (1, E), 1)
-
-    def sweep(k, _):
-        here = lane == k
-        for i in range(len(shifts)):
-            now = inv[i]
-            row = inv[i, pl.ds(k, 1), :]
-            col = jnp.sum(jnp.where(here, now, 0.0), axis=1, keepdims=True)
-            pivot = 1.0 / jnp.sum(jnp.where(here, row, 0.0), axis=1, keepdims=True)
-            row = jnp.where(here, -pivot, row * pivot)
-            inv[i] = jnp.where(here, 0.0, now) - col * row
-            inv[i, pl.ds(k, 1), :] = row
-        return 0
-
-    lax.fori_loop(0, E, sweep, 0)
+    place = lax.broadcasted_iota(jnp.int32, (8, 1), 0)
+    count = len(shifts)
+
+    def sweep(n, _):
+        at = pl.multiple_of(n * 8, 8)
+        before = [inv[i, pl.ds(at, 8), :] for i in range(count)]
+        panel = list(before)
+        for k in range(8):
+            here = lane == at + k
+            for i in range(count):
+                now = panel[i]
+                col = jnp.sum(jnp.where(here, now, 0.0), axis=1, keepdims=True)
+                pivot = 1.0 / col[k : k + 1]
+                row = jnp.where(here, -pivot, now[k : k + 1] * pivot)
+                panel[i] = jnp.where(place == k, row, jnp.where(here, 0.0, now) - col * row)
+        inside = (lane >= at) & (lane < at + 8)
+        for i in range(count):
+            change = lax.dot_general(
+                before[i], panel[i], (((0,), (0,)), ((), ())), precision=HIGH,
+                preferred_element_type=jnp.float32,
+            )
+            inv[i] = jnp.where(inside, 0.0, inv[i]) - change
+            inv[i, pl.ds(at, 8), :] = panel[i]
+        return 0
+
+    lax.fori_loop(0, E // 8, sweep, 0)
     root = 0.125 * eye
     for i, weight in enumerate(weights):
         root = root - weight * inv[i]
@@ -250,52 +274,76 @@
     transform = transform - jnp.sum(transform, axis=0, keepdims=True) * (1.0 / E) + 1.0 / E
     turned = transform.T
 
-    for one in slab_copies:
-        one.wait_recv()
-    back_copies = [
-        copy(mixed.at[peer("runner", k)], back.at[pl.ds(2 + r * S, S)], back_s.at[k - 1], back_r.at[k - 1],
-             "runner", peer("runner", k))
-        for k in range(1, R)
-    ]
+    lax.fori_loop(0, chunks, wait_slabs, 0)
+
+    def back_copies(c):
+        return [
+            copy(mixed.at[peer("runner", k), c], back.at[c, pl.ds(2 + r * S, S)], back_s.at[k - 1, c],
+                 back_r.at[k - 1, c], "runner", peer("runner", k))
+            for k in range(1, R)
+        ]
+
     for j in range(S):
         for f in range(fields):
             value = slab[:, :, j, f].reshape(E, C)
             result = jnp.dot(turned, value, precision=HIGH, preferred_element_type=jnp.float32)
-            mixed[:, j, f] = result.reshape(R, M, C)
-    for one in back_copies:
-        one.start()
-    back[pl.ds(2 + r * S, S)] = mixed[r]
-    for one in back_copies:
-        one.wait_recv()
-
-    last_copies = [
-        copy(back.at[pl.ds(2, 2)], back.at[pl.ds(rows + 2, 2)], last_s.at[0], last_r.at[0], "tile", down),
-        copy(back.at[pl.ds(rows, 2)], back.at[pl.ds(0, 2)], last_s.at[1], last_r.at[1], "tile", up),
-    ]
-    for one in last_copies:
-        one.start()
-    for one in last_copies:
-        one.wait_recv()
-
-    def last_row(n, _):
-        j = n // chunks
-        members = pl.ds(pl.multiple_of((n % chunks) * mch, mch), mch)
-        rates = tendency_row(lambda d, f: back[j + 2 + d, f, members, :])
-        for f, rate in enumerate(rates):
-            out[j, f, members, :] = back[j + 2, f, members, :] + TIME_STEP * rate
-        return 0
-
-    lax.fori_loop(0, rows * chunks, last_row, 0)
+            mixed[:, :, j, f] = result.reshape(R, chunks, mch, C)
+
+    def give_back(c, _):
+        for one in back_copies(c):
+            one.start()
+        back[c, pl.ds(2 + r * S, S)] = mixed[r, c]
+        return 0
+
+    lax.fori_loop(0, chunks, give_back, 0)
+
+    def last_copies(c):
+        return (
+            copy(back.at[c, pl.ds(2, 2)], back.at[c, pl.ds(rows + 2, 2)], last_s.at[0, c], last_r.at[0, c],
+                 "tile", down),
+            copy(back.at[c, pl.ds(rows, 2)], back.at[c, pl.ds(0, 2)], last_s.at[1, c], last_r.at[1, c],
+                 "tile", up),
+        )
+
+    def last_begin(c, _):
+        for one in back_copies(c):
+            one.wait_recv()
+        for one in last_copies(c):
+            one.start()
+        return 0
+
+    def last_end(c, _):
+        for one in last_copies(c):
+            one.wait_recv()
+
+        def last_row(j, _):
+            rates = tendency_row(lambda d, f: back[c, j + 2 + d, f])
+            for f, rate in enumerate(rates):
+                out[c, j, f] = back[c, j + 2, f] + TIME_STEP * rate
+            return 0
+
+        lax.fori_loop(0, rows, last_row, 0)
+        return 0
+
+    def last_both(c, _):
+        last_begin(c, 0)
+        last_end(c - 1, 0)
+        return 0
+
+    last_begin(0, 0)
+    lax.fori_loop(1, chunks, last_both, 0)
+    last_end(chunks - 1, 0)
 
     def drain(c, _):
         for s in range(4):
             for one in halos(s, c):
                 one.wait_send()
+        for one in (*slab_copies(c), *back_copies(c), *last_copies(c)):
+            one.wait_send()
         return 0
 
     lax.fori_loop(0, chunks, drain, 0)
-    for group in (cell_copies, pick_copies, first_copies, second_copies, third_copies,
-                  slab_copies, back_copies, last_copies):
+    for group in (cell_copies, pick_copies, first_copies, second_copies, third_copies):
         for one in group:
             one.wait_send()
 
@@ -316,7 +364,7 @@
     pairs = lambda n: [dma((n,)), dma((n,))]
     result = pl.pallas_call(
         functools.partial(kernel, R, T),
-        out_shape=jax.ShapeDtypeStruct((rows, fields, M, C), f32),
+        out_shape=jax.ShapeDtypeStruct((chunks, rows, fields, mch, C), f32),
         in_specs=[vmem] * 4,
         out_specs=vmem,
         scratch_shapes=[
@@ -331,18 +379,19 @@
             pltpu.VMEM((R, h, E + 128), f32),
             pltpu.VMEM((T, h, E + 128), f32),
             pltpu.VMEM((4, E, E), f32),
-            pltpu.VMEM((R, S, fields, M, C), f32),
-            pltpu.VMEM((rows + 4, fields, M, C), f32),
+            pltpu.VMEM((R, chunks, S, fields, mch, C), f32),
+            pltpu.VMEM((chunks, rows + 4, fields, mch, C), f32),
             dma((4, 2, chunks)), dma((4, 2, chunks)),
             *pairs(R - 1), *pairs(R - 1), *pairs(T - 1), *pairs(R - 1), *pairs(T - 1),
-            *pairs(R - 1), *pairs(R - 1), *pairs(2),
+            dma((R - 1, chunks)), dma((R - 1, chunks)), dma((R - 1, chunks)), dma((R - 1, chunks)),
+            dma((2, chunks)), dma((2, chunks)),
         ],
         compiler_params=pltpu.CompilerParams(
             collective_id=0, has_side_effects=True, vmem_limit_bytes=48 * 1024 * 1024
         ),
         name="forecast",
     )(start, obs_cell[0], obs_value[0], obs_var[0])
-    return result.transpose(2, 1, 0, 3)
+    return result.transpose(0, 3, 2, 1, 4).reshape(M, fields, rows, C)
 
 
 def solution(mesh):

time: 165 us -> 135 us (0.82)
  Pallas kernels: 159 us -> 131 us
    pallas_call x1, Pallas kernels: 159 us -> 131 us  [per_device(): pl.pallas_call(functools.partial(kernel, R, T), out_shape=jax.ShapeDtypeS...]
where the time goes in v2:
time: 135 us
  Pallas kernels  131 us (97%)
  local copies, waits for them, and re-layouts  2.99 us (2%)
  other arithmetic  1.57 us (1%)
    pallas_call x1, Pallas kernels, per_device(): pl.pallas_call(functools.partial(kernel, R, T), out_shape=jax.ShapeDtypeS...  131 us

profile of v2, /device:TPU:29, one launch (start us, length us, event | category | flops | bytes accessed | tf_op | source)
XLA Modules:
  0.0 135.2 jit_solution(621336724706025690)
XLA Ops:
  0.0 1.6 %broadcast_add_fusion = f32[32,3,8,512]{3,2,1,0:T(8,128)S(1)} fusion(f32[32,3,8,512]{3,2,1,0:T(8,128)} %param.6, f32[3,8,512]{2,1,0:T(8,128)} %param.5), kind=kLoop, calls=%fused_computation.1 | loop fusion | flops 393216 | bytes 3194880 | tf_op jit(solution)/shard_map/add | solution.py:359
  1.6 0.0 copy-start
  1.6 0.0 copy-start.1
  1.6 0.0 copy-start.2
  1.6 0.9 copy.9
  2.5 0.0 copy-done
  2.5 0.0 copy-done.1
  2.6 0.0 copy-done.2
  2.6 130.5 %forecast.1 = f32[4,8,3,8,512]{4,3,2,1,0:T(8,128)S(1)} custom-call(f32[4,8,3,8,512]{4,3,2,1,0:T(8,128)S(1)} %bitcast.9, s32[1,256]{1,0:T(1,128)S(1)} %bitcast.11, f32[1,256]{1,0:T(1,128)S(1)} %bitcast.12, f32[1,256]{1,0:T(1,128)S(1)} %bitcast.13), custom_call_target="tpu_custom_call" | custom-call | tf_op jit(solution)/shard_map/forecast/pallas_call | solution.py:365
  133.1 2.1 %copy.7 = f32[4,8,3,8,512]{4,3,2,1,0:T(8,128)} copy(f32[4,8,3,8,512]{4,1,2,3,0:T(8,128)S(1)} %bitcast.10) | data formatting | bytes 3145728 | tf_op jit(solution)/shard_map/transpose | solution.py:394
Async XLA Ops:
  1.6 1.0 copy-start
  1.6 1.0 copy-start.1
  1.6 1.0 copy-start.2

commit v3 on v2

--- a/solution.py
+++ b/solution.py
@@ -67,6 +67,7 @@
     S = rows // R
     obs = cell.shape[-1]
     h = E // T
+    early = min(1, chunks)
     up = lax.rem(t + 1, T)
     down = lax.rem(t + T - 1, T)
 
@@ -154,7 +155,12 @@
                 slab[r, c] = own[c, pl.ds(r * S, S)]
             return 0
 
-        lax.fori_loop(0, chunks, stage, 0)
+        if s < 3:
+            lax.fori_loop(0, chunks, stage, 0)
+        else:
+            lax.fori_loop(0, early, stage, 0)
+            lax.fori_loop(0, early, start_slabs, 0)
+            lax.fori_loop(early, chunks, stage, 0)
 
     for one in cell_copies:
         one.wait_recv()
@@ -227,7 +233,7 @@
     for one in third_copies:
         one.start()
 
-    lax.fori_loop(0, chunks, start_slabs, 0)
+    lax.fori_loop(early, chunks, start_slabs, 0)
     for one in third_copies:
         one.wait_recv()
 

time: 135 us -> 127 us (0.941)
  Pallas kernels: 131 us -> 122 us
    pallas_call x1, Pallas kernels: 131 us -> 122 us  [per_device(): pl.pallas_call(functools.partial(kernel, R, T), out_shape=jax.ShapeDtypeS...]
where the time goes in v3:
time: 127 us
  Pallas kernels  122 us (96%)
  local copies, waits for them, and re-layouts  2.99 us (2%)
  other arithmetic  1.57 us (1%)
    pallas_call x1, Pallas kernels, per_device(): pl.pallas_call(functools.partial(kernel, R, T), out_shape=jax.ShapeDtypeS...  122 us

profile of v3, /device:TPU:29, one launch (start us, length us, event | category | flops | bytes accessed | tf_op | source)
XLA Modules:
  0.0 126.8 jit_solution(17866072987420014596)
XLA Ops:
  0.0 1.6 %broadcast_add_fusion = f32[32,3,8,512]{3,2,1,0:T(8,128)S(1)} fusion(f32[32,3,8,512]{3,2,1,0:T(8,128)} %param.6, f32[3,8,512]{2,1,0:T(8,128)} %param.5), kind=kLoop, calls=%fused_computation.1 | loop fusion | flops 393216 | bytes 3194880 | tf_op jit(solution)/shard_map/add | solution.py:365
  1.6 0.0 copy-start
  1.6 0.0 copy-start.1
  1.6 0.0 copy-start.2
  1.6 0.9 copy.9
  2.5 0.0 copy-done
  2.5 0.0 copy-done.1
  2.6 0.0 copy-done.2
  2.6 122.2 %forecast.1 = f32[4,8,3,8,512]{4,3,2,1,0:T(8,128)S(1)} custom-call(f32[4,8,3,8,512]{4,3,2,1,0:T(8,128)S(1)} %bitcast.9, s32[1,256]{1,0:T(1,128)S(1)} %bitcast.11, f32[1,256]{1,0:T(1,128)S(1)} %bitcast.12, f32[1,256]{1,0:T(1,128)S(1)} %bitcast.13), custom_call_target="tpu_custom_call" | custom-call | tf_op jit(solution)/shard_map/forecast/pallas_call | solution.py:371
  124.7 2.1 %copy.7 = f32[4,8,3,8,512]{4,3,2,1,0:T(8,128)} copy(f32[4,8,3,8,512]{4,1,2,3,0:T(8,128)S(1)} %bitcast.10) | data formatting | bytes 3145728 | tf_op jit(solution)/shard_map/transpose | solution.py:400
Async XLA Ops:
  1.6 1.0 copy-start
  1.6 1.0 copy-start.1
  1.6 1.0 copy-start.2
